TPU v7x, 512 devices: a whole 4x4x16 slice. The times are simulated.
512 devices in a mesh: dp: 64 (over z, x), tensor: 8 (over y, core).
Axes of the slice: x: 4, y: 4, z: 16, core: 2. Of those that a mesh axis runs over, the one named last changes fastest.
Arguments:
- grad: bfloat16 [16, 512, 16384], P(None, 'dp', 'tensor'), may hold values from -40 to 40
- owner: int32 [16, 32], replicated, may hold values from 0 to 63, as said below
- left_root: bfloat16 [8, 192, 512, 512], P('tensor', 'dp'), may hold values from -0.5 to 4.5
- right_root: bfloat16 [8, 192, 512, 512], P('tensor', 'dp'), may hold values from -0.5 to 4.5
Outputs:
- direction: bfloat16 [16, 512, 16384], P(None, 'dp', 'tensor')
- update_rms: float32 [], replicated
Inputs may be any that keep to these rules, and one draw needn't show every extreme that they name: `owner`: among the 16 x 4 blocks of each tensor index, no dp index owns more than 3, and some dp index owns exactly 3.
All inputs are finite; a program needn't handle non-finite values.
Results may differ from a plain program's by a relative error of at most 0.0049.
Values may be sent and summed in bfloat16 or wider, within the bound.
A program may use at most 64 MiB of HBM per device.

v0:
```python
import jax
import jax.numpy as jnp
from jax import lax
from jax.sharding import PartitionSpec as P

BLK = 512


EPSILON = 1e-06


def precondition(block, left_factor, right_factor):
    left_part = jnp.dot(left_factor, block, preferred_element_type=jnp.float32).astype(jnp.bfloat16)
    product = jnp.dot(left_part, right_factor, preferred_element_type=jnp.float32)
    grad_mean = jnp.mean(jnp.square(block.astype(jnp.float32)))
    prod_mean = jnp.mean(jnp.square(product))
    update = product * (jnp.sqrt(grad_mean + EPSILON) / jnp.sqrt(prod_mean + EPSILON))
    return (update, jnp.sum(update * update))


def process_slot(block, left_factor, right_factor):
    return precondition(block, left_factor, right_factor)


def slot_numbers(owners_here, dp_size):
    onehot = (owners_here[..., None] == jnp.arange(dp_size, dtype=jnp.int32)).astype(jnp.int32)
    before = jnp.cumsum(onehot, axis=-2) - onehot
    return jnp.sum(before * onehot, axis=-1)


def global_scale(partial_sum, cells):
    squares = lax.psum(partial_sum, ("dp", "tensor"))
    update_rms = jnp.sqrt(squares / cells + EPSILON)
    return (1.0 / update_rms, update_rms)


def per_device(grad, owner, left_root, right_root):
    row_blocks, piece_rows, width = grad.shape
    dp_size = lax.axis_size("dp")
    slot_count = left_root.shape[1]
    col_blocks = width // BLK
    per_group = row_blocks * col_blocks
    tensor_index = lax.axis_index("tensor")
    owners_here = lax.dynamic_slice_in_dim(owner, tensor_index * col_blocks, col_blocks, 1).reshape(
        per_group
    )
    slot_of = slot_numbers(owners_here, dp_size)
    position = slot_of * dp_size + owners_here
    select = (
        position[None, :] == jnp.arange(slot_count * dp_size, dtype=jnp.int32)[:, None]
    ).astype(jnp.bfloat16)
    pieces = (
        grad.reshape(row_blocks, piece_rows, col_blocks, BLK)
        .transpose(0, 2, 1, 3)
        .reshape(per_group, piece_rows * BLK)
    )
    outgoing = jnp.dot(select, pieces, preferred_element_type=jnp.float32).astype(jnp.bfloat16)
    outgoing = outgoing.reshape(slot_count, dp_size * piece_rows, BLK)
    left_factor = left_root[0]
    right_factor = right_root[0]
    cells = row_blocks * BLK * width * lax.axis_size("tensor")
    arrived = lax.all_to_all(outgoing, "dp", split_axis=1, concat_axis=1, tiled=True)
    outcomes = [
        process_slot(arrived[slot_index], left_factor[slot_index], right_factor[slot_index])
        for slot_index in range(slot_count)
    ]
    updates = jnp.stack([outcome[0] for outcome in outcomes])
    partial_sum = sum([outcome[1] for outcome in outcomes])
    inv_rms, update_rms = global_scale(partial_sum, cells)
    returned = lax.all_to_all(
        (updates * inv_rms).astype(jnp.bfloat16), "dp", split_axis=1, concat_axis=1, tiled=True
    )
    flat = returned.reshape(slot_count * dp_size, piece_rows * BLK)
    placed = jnp.take(flat, position, axis=0)
    direction = placed
    direction = (
        direction.reshape(row_blocks, col_blocks, piece_rows, BLK)
        .transpose(0, 2, 1, 3)
        .reshape(row_blocks, piece_rows, width)
    )
    return (direction, update_rms)


def solution(mesh):
    return jax.shard_map(
        per_device,
        mesh=mesh,
        in_specs=(
            P(None, "dp", "tensor"),
            P(),
            P("tensor", "dp", None, None),
            P("tensor", "dp", None, None),
        ),
        out_specs=(P(None, "dp", "tensor"), P()),
        check_vma=False,
    )
```

profile of v0, /device:TPU:1, one launch (start us, length us, event | category | flops | bytes accessed | tf_op | source)
XLA Modules:
  0.0 363.3 jit_solution(16167675106791899852)
XLA Ops:
  0.6 0.8 constant_dynamic-slice_fusion
  1.4 0.1 eq.28
  1.5 0.1 fusion.23
  1.6 0.1 reduce_window_sum.11
  1.7 0.2 select_reduce_fusion
  1.9 1.2 copy.18
  3.1 0.6 convolution_convert_fusion
  3.6 0.8 reshape.89
  4.4 1.4 copy.9
  5.8 113.8 %all_to_all.10 = bf16[3,512,512]{2,0,1:T(4,128)(2,1)S(1)} all-to-all(bf16[3,512,512]{2,0,1:T(4,128)(2,1)S(1)} %copy.9), channel_id=1, replica_groups=mesh['dp'=64,'tensor'=8] {'dp'}, dimensions={1} | all-to-all | bytes 3145728 | tf_op jit(solution)/shard_map/all_to_all | solution.py:62
  119.6 2.2 fusion.26
  121.8 0.9 multiply_reduce_fusion.8
  122.7 3.7 %multiply_reduce_fusion.7 = (f32[]{:T(128)}, f32[512,512]{1,0:T(8,128)}) fusion(bf16[1,3,512,512]{3,2,1,0:T(8,128)(2,1)} %param.7, bf16[1,3,512,512]{3,2,1,0:T(8,128)(2,1)} %param.6, bf16[1,512,512]{2,0,1:T(2,128)(2,1)S(1)} %get-tuple-element.2), kind=kOutput, calls=%fused_computation.17 | convolution fusion | flops 537657344 | bytes 2621444 | tf_op jit(solution)/shard_map/dot_general | solution.py:14
  126.4 2.8 multiply_reduce_fusion.5
  129.2 0.9 multiply_reduce_fusion.4
  130.1 0.0 copy-start
  130.1 3.8 %multiply_reduce_fusion.3 = (f32[]{:T(128)}, f32[512,512]{1,0:T(8,128)}) fusion(bf16[1,3,512,512]{3,2,1,0:T(8,128)(2,1)} %param.7, bf16[1,3,512,512]{3,2,1,0:T(8,128)(2,1)} %param.6, bf16[1,512,512]{2,0,1:T(2,128)(2,1)S(1)} %get-tuple-element.4), kind=kOutput, calls=%fused_computation.13 | convolution fusion | flops 537657344 | bytes 2621444 | tf_op jit(solution)/shard_map/dot_general | solution.py:14
  137.9 0.0 copy-done
  137.9 0.9 multiply_reduce_fusion.2
  138.8 0.9 multiply_reduce_fusion.1
  140.9 2.1 multiply_reduce_fusion
  143.7 105.6 %psum.7 = f32[]{:T(128)} all-reduce(f32[]{:T(128)S(6)} %add.87), channel_id=1, replica_groups=mesh['dp'=64,'tensor'=8] {'dp','tensor'}, use_global_device_ids=true, to_apply=%region_11.12 | all-reduce | flops 1 | bytes 8 | tf_op jit(solution)/shard_map/psum | solution.py:32
  250.1 0.4 fusion
  250.5 2.7 copy.13
  253.2 0.0 copy-start.1
  253.2 7.9 %all-to-all-start.1 = ((bf16[3,512,512]{2,0,1:T(4,128)(2,1)}), bf16[3,512,512]{2,0,1:T(4,128)(2,1)S(1)}, u32[]{:S(2)}, u32[]{:S(2)}) async-start(bf16[3,512,512]{2,0,1:T(4,128)(2,1)} %copy.13), calls=%async_computation.1 | async-start | bytes 4194304 | tf_op jit(solution)/shard_map/all_to_all | solution.py:70
  261.2 0.1 reshape.91
  261.2 0.1 mul.69
  261.4 0.0 copy-done.1
  261.4 0.1 compare_and_fusion
  261.5 94.6 %all-to-all-done.1 = bf16[3,512,512]{2,0,1:T(4,128)(2,1)S(1)} async-done(((bf16[3,512,512]{2,0,1:T(4,128)(2,1)}), bf16[3,512,512]{2,0,1:T(4,128)(2,1)S(1)}, u32[]{:S(2)}, u32[]{:S(2)}) %all-to-all-start.1) | async-done | bytes 1572896 | tf_op jit(solution)/shard_map/all_to_all | solution.py:70
  356.1 1.5 copy.14
  357.6 2.6 reshape.90
  360.2 0.9 gather_fusion
  361.1 0.2 copy.19
  361.3 0.9 broadcast_select_fusion
  (3 shorter events, 0.0 us)
Async XLA Ops:
  130.1 7.8 %copy-start = (f32[512,512]{1,0:T(8,128)S(1)}, f32[512,512]{1,0:T(8,128)}, u32[]{:S(2)}) copy-start(f32[512,512]{1,0:T(8,128)} %get-tuple-element.18) | copy-start | bytes 3145732
  253.2 8.1 %copy-start.1 = (s32[16,32]{1,0:T(8,128)S(1)}, s32[16,32]{1,0:T(8,128)}, u32[]{:S(2)}) copy-start(s32[16,32]{1,0:T(8,128)} %param.5) | copy-start | bytes 6148
  253.2 102.9 %all-to-all-start.1 = ((bf16[3,512,512]{2,0,1:T(4,128)(2,1)}), bf16[3,512,512]{2,0,1:T(4,128)(2,1)S(1)}, u32[]{:S(2)}, u32[]{:S(2)}) async-start(bf16[3,512,512]{2,0,1:T(4,128)(2,1)} %copy.13), calls=%async_computation.1 | async-start | bytes 4194304 | tf_op jit(solution)/shard_map/all_to_all | solution.py:70
where the time goes:
time: 369 us; the launch traced here: 363 us
  blocking collectives  219 us (59%)
  waiting for transfers between devices  94.6 us (26%)
  local copies, waits for them, and re-layouts  14.5 us (4%)
  matrix products  10.9 us (3%)
  between operations  8.51 us (2%)
  starting transfers between devices  7.94 us (2%)
  other arithmetic  7.45 us (2%)
    all_to_all x1, blocking collectives, per_device(): lax.all_to_all(outgoing, 'dp', split_axis=1, concat_axis=1, tiled=True)  114 us
    psum x1, blocking collectives, global_scale(): squares = lax.psum(partial_sum, ('dp', 'tensor'))  106 us
    all_to_all x1, waiting for transfers between devices, per_device(): lax.all_to_all((updates * inv_rms).astype(jnp.bfloat16), 'dp', split_axis...  94.6 us
    dot_general x3, matrix products, precondition(): jnp.dot(left_part, right_factor, preferred_element_type=jnp.float32)  10.4 us
    all_to_all x1, starting transfers between devices, per_device(): lax.all_to_all((updates * inv_rms).astype(jnp.bfloat16), 'dp', split_axis...  7.94 us
  transfers between devices with their start and end apart: 1, of which 1 were waited for; matrix products, arithmetic and copies ran while one was open for 0% of the time, Pallas kernels for 0%

commit v1 on v0

v1 whole, which is shorter than its diff:
```python
import functools

import jax
import jax.numpy as jnp
from jax import lax
from jax.experimental import pallas as pl
from jax.experimental.pallas import tpu as pltpu
from jax.sharding import PartitionSpec as P

BLK = 512
EPSILON = 1e-06
MESH = pl.DeviceIdType.MESH

NX = 4
SLOTS = 3
CELLS = NX * SLOTS
CHUNKS = 2
CAPACITY = (43, 38, 35, 29, 25, 20, 13, 8)


def block_cells(owners):
    n = owners.shape[-1]
    index = jnp.arange(n, dtype=jnp.int32)
    same = owners[:, :, None] == owners[:, None, :]
    slot = jnp.sum((same & (index[None, :] < index[:, None])).astype(jnp.int32), axis=-1)
    cell = owners * SLOTS + slot
    rank = jnp.sum((cell[:, None, :] < cell[:, :, None]).astype(jnp.int32), axis=-1)
    return cell, rank


def plane_split(cell, planes, capacity):
    n = cell.shape[-1]
    hops = len(capacity)
    planes_of = cell // CELLS
    z = jnp.arange(planes, dtype=jnp.int32)
    distance = (planes_of[:, None, :] - z[None, :, None]) % planes
    steps = jnp.arange(planes + 1, dtype=jnp.int32)
    nearer = jnp.sum((distance[:, :, None, :] < steps[None, None, :, None]).astype(jnp.int32), axis=-1)
    room = jnp.array(tuple(capacity) + (0,), jnp.int32)
    up_limit = jnp.min(nearer[:, :, 1 : hops + 2] + room, axis=-1)
    down_limit = jnp.max(nearer[:, :, planes - hops : planes + 1][:, :, ::-1] - room, axis=-1)
    local = nearer[:, :, 1]
    fits = jnp.all(down_limit <= up_limit)
    cut = jnp.clip((down_limit + up_limit) // 2, local, n)
    starts = jnp.sum((planes_of[:, None, :] < z[None, :, None]).astype(jnp.int32), axis=-1)
    return starts + cut, cut - local, fits


def make_table(cell, rank, ends, ups, devices):
    n = cell.shape[0]
    index = jnp.arange(n, dtype=jnp.int32)
    hit = (rank[None, :] == index[:, None]).astype(jnp.int32)
    block_of = jnp.sum(hit * index[None, :], axis=-1)
    cell_of = jnp.sum(hit * cell[None, :], axis=-1)
    cells = jnp.arange(devices * SLOTS, dtype=jnp.int32)
    below = jnp.sum((cell[None, :] < cells[:, None]).astype(jnp.int32), axis=-1)
    return jnp.concatenate([block_of, cell_of, rank, below, ends, ups])


def fold(piece):
    return jnp.concatenate([piece[:, :128], piece[:, 128:]], axis=0).astype(jnp.bfloat16)


def loop(count, body, unroll):
    turns = count // unroll

    def turn(t, carry):
        for u in range(unroll):
            body(t * unroll + u)
        return carry

    if turns:
        lax.fori_loop(0, turns, turn, 0)
    for j in range(turns * unroll, count):
        body(j)


def kernel(planes, nblk, capacity, *refs):
    hops = len(capacity)
    names = iter(refs)

    def take(*shape):
        if not shape:
            return next(names)
        return [take(*shape[1:]) for _ in range(shape[0])]

    tab, grad, left_hbm, right_hbm = take(4)
    out, ssq_out = take(2)
    left, right, mats, halves, prods, scales, squares = take(7)
    folded = take(CHUNKS)
    first = take(2, CHUNKS)
    ring = take(hops - 1, 2, CHUNKS)
    ring_last = take(CHUNKS)
    xs, xr, ys = take(3)
    back_send = take(hops, 2, CHUNKS)
    back = take(hops - 1, 2, CHUNKS)
    back_first = take(CHUNKS)
    back_last = take(CHUNKS)
    load_sem, ring_ss, ring_rs, x_ss, x_rs, y_ss, y_rs, back_ss, back_rs = take(9)

    rows = mats.shape[1]
    dp = lax.axis_index("dp")
    tensor = lax.axis_index("tensor")
    z, x = dp // NX, dp % NX
    devices = planes * NX
    per_row = nblk // grad.shape[0]
    CELL_OF, RANK_OF, BELOW = nblk, 2 * nblk, 3 * nblk
    ENDS = BELOW + devices * SLOTS
    UPS = ENDS + planes

    def plane(delta):
        return (z + (delta + planes)) % planes

    def device(zz, xx):
        return (zz * NX + xx, tensor)

    toward = [device(plane(1), x), device(plane(-1), x)]
    along = [None] + [device(z, (x + rel) % NX) for rel in range(1, NX)]

    factors = [
        pltpu.make_async_copy(left_hbm.at[0], left, load_sem.at[0]),
        pltpu.make_async_copy(right_hbm.at[0], right, load_sem.at[1]),
    ]
    for copy in factors:
        copy.start()

    barrier = pltpu.get_barrier_semaphore()
    peers = toward + along[1:]
    for peer in peers:
        pl.semaphore_signal(barrier, inc=1, device_id=peer, device_id_type=MESH)

    def fold_row(r):
        for c in range(per_row):
            piece = grad[r, :, pl.ds(c * BLK, BLK)].astype(jnp.float32)
            for h in range(CHUNKS):
                folded[h][r * per_row + c] = fold(piece[:, h * 256 : (h + 1) * 256])

    loop(grad.shape[0], fold_row, 2)

    end = tab[ENDS + z]

    def fill_first(j):
        for d, r in ((0, (end - 1 - j) & (nblk - 1)), (1, (end + j) & (nblk - 1))):
            block = tab[r]
            for h in range(CHUNKS):
                first[d][h][j] = folded[h][block]

    loop(capacity[0], fill_first, 4)

    pl.semaphore_wait(barrier, len(peers))

    sends = []

    def remote(src, dst, ss, rs, target):
        copy = pltpu.make_async_remote_copy(
            src_ref=src, dst_ref=dst, send_sem=ss, recv_sem=rs, device_id=target, device_id_type=MESH
        )
        copy.start()
        sends.append(copy)
        return copy

    ring_copies = {}

    def ring_at(k, d, h):
        if k < hops:
            return ring[k - 1][d][h]
        return ring_last[h].at[pl.ds(d * capacity[k - 1], capacity[k - 1])]

    def send_ring(k, d, h):
        src = first[d][h] if k == 1 else ring_at(k - 1, d, h).at[pl.ds(0, capacity[k - 1])]
        ring_copies[k, d, h] = remote(
            src, ring_at(k, d, h), ring_ss.at[k - 1, d, h], ring_rs.at[k - 1, d, h], toward[d]
        )

    for h in range(CHUNKS):
        for d in range(2):
            send_ring(1, d, h)

    x_copies = {}

    def send_x(delta, h):
        x_copies[delta, h] = [
            remote(xs.at[delta, h, rel], xr.at[delta, h, rel], x_ss.at[delta, h, rel], x_rs.at[delta, h, rel], along[rel])
            for rel in range(1, NX)
        ]

    def put_x(delta, h, rel, s, value):
        if rel == 0:
            xr[delta, h, 0, s] = value
        else:
            xs[delta, h, rel, s] = value

    def cell_index(rel, s):
        return z * CELLS + ((x + rel) % NX) * SLOTS + s

    for rel in range(NX):
        for s in range(SLOTS):
            rank = tab[BELOW + cell_index(rel, s)]
            block = tab[jnp.minimum(rank, nblk - 1)]
            for h in range(CHUNKS):
                put_x(0, h, rel, s, folded[h][block])
    for h in range(CHUNKS):
        send_x(0, h)

    def pick(delta, h):
        source = plane(-delta)
        source_end, source_ups = tab[ENDS + source], tab[UPS + source]
        k = min(delta, planes - delta)
        room = capacity[k - 1]
        for rel in range(NX):
            for s in range(SLOTS):
                rank = tab[BELOW + cell_index(rel, s)]
                up = (source_end - 1 - rank) & (nblk - 1)
                down = (rank - source_end) & (nblk - 1)
                if k == hops:
                    at = jnp.where(up < source_ups, jnp.minimum(up, room - 1), room + jnp.minimum(down, room - 1))
                    value = ring_last[h][at]
                elif delta < hops:
                    value = ring[k - 1][0][h][jnp.minimum(up, room - 1)]
                else:
                    value = ring[k - 1][1][h][jnp.minimum(down, room - 1)]
                put_x(delta, h, rel, s, value)
        send_x(delta, h)

    squares[...] = jnp.zeros_like(squares)

    def place(delta, h):
        for copy in x_copies[delta, h]:
            copy.wait_recv()
        source = plane(-delta)
        for s in range(SLOTS):
            total = None
            for pair in range(NX // 2):
                low, high = (
                    xr[delta, h, (x - (2 * pair + i) + NX) % NX, s].astype(jnp.float32) for i in range(2)
                )
                term = low * low + high * high
                total = term if total is None else total + term
                at = pl.ds(pl.multiple_of(source * (8 * NX) + 16 * pair, 16), 16)
                mats[s, at, pl.ds(h * 256, 128)] = jnp.concatenate([low[:8], high[:8]], 0).astype(jnp.bfloat16)
                mats[s, at, pl.ds(h * 256 + 128, 128)] = jnp.concatenate([low[8:], high[8:]], 0).astype(jnp.bfloat16)
            squares[s] += total

    pending = [(0, h) for h in range(CHUNKS)]
    for k in range(1, hops + 1):
        for h in range(CHUNKS):
            for d in range(2):
                ring_copies[k, d, h].wait_recv()
                if k < hops:
                    send_ring(k + 1, d, h)
            ready = []
            for delta in sorted({k, planes - k}):
                ready.append((delta, h))
            for delta, hh in ready:
                pick(delta, hh)
            while len(pending) > 4:
                place(*pending.pop(0))
            pending += ready
    for copy in factors:
        copy.wait()
    for h in range(CHUNKS):
        for item in [p for p in pending if p[1] == h]:
            place(*item)

        def left_part(s, carry):
            part = jnp.dot(left[s], mats[s, :, pl.ds(h * 256, 256)], preferred_element_type=jnp.float32)
            halves[s, :, pl.ds(h * 256, 256)] = part.astype(jnp.bfloat16)
            return carry

        lax.fori_loop(0, SLOTS, left_part, 0)

    cells = rows * BLK

    def right_part(s, total):
        product = jnp.dot(halves[s], right[s], preferred_element_type=jnp.float32)
        prods[s] = product
        prod_sum = jnp.sum(product * product, keepdims=True)
        grad_sum = jnp.sum(squares[s], keepdims=True)
        scale = jnp.sqrt(grad_sum / cells + EPSILON) / jnp.sqrt(prod_sum / cells + EPSILON)
        scales[s] = jnp.broadcast_to(scale, (8, 128))
        own = tab[BELOW + dp * SLOTS + s]
        found = jnp.full((1, 1), tab[CELL_OF + jnp.minimum(own, nblk - 1)])
        held = found == jnp.full((1, 1), dp * SLOTS + s)
        return total + jnp.where(held, prod_sum * scale * scale, 0.0)

    total = lax.fori_loop(0, SLOTS, right_part, jnp.zeros((1, 1), jnp.float32))
    ssq_out[...] = jnp.broadcast_to(total, ssq_out.shape)

    y_copies = {}

    def y_at(delta, h):
        if delta == 0:
            return back_last[h], 2 * capacity[0]
        if delta == hops:
            return back_first[h], 0
        k, d = (delta, 1) if delta < hops else (planes - delta, 0)
        return back[k - 1][d][h], capacity[k]

    def send_y(delta):
        target = plane(delta)
        for s in range(SLOTS):
            scale = scales[s][:, :1]
            for rel in range(NX):
                xx = (x + rel) % NX
                value = prods[s, pl.ds(pl.multiple_of((target * NX + xx) * 8, 8), 8), :] * scale
                for h in range(CHUNKS):
                    part = fold(value[:, h * 256 : (h + 1) * 256])
                    if rel == 0:
                        ref, row = y_at(delta, h)
                        ref[row + x * SLOTS + s] = part
                    else:
                        ys[delta, h, rel, s] = part
        for h in range(CHUNKS):
            ref, row = y_at(delta, h)
            y_copies[delta, h] = [
                remote(
                    ys.at[delta, h, rel], ref.at[pl.ds(row + x * SLOTS, SLOTS)],
                    y_ss.at[delta, h, rel], y_rs.at[delta, h, rel], along[rel],
                )
                for rel in range(1, NX)
            ]

    def wait_y(delta, h):
        for copy in y_copies.pop((delta, h), ()):
            copy.wait_recv()

    back_copies = {}

    def send_back(k, d, h):
        if k < hops:
            back_copies[k + 1, d, h].wait_recv()
        delta = planes - k if d == 0 else k
        wait_y(delta, h)
        target_end = tab[ENDS + plane(delta)]
        low = z * CELLS
        width = capacity[k - 1]
        filled = capacity[k] if k < hops else 0

        ref, row = y_at(delta, h)

        def merge(j, keep):
            rank = (target_end - 1 - j if d == 0 else target_end + j) & (nblk - 1)
            local = tab[CELL_OF + rank] - low
            at = row + jnp.clip(local, 0, CELLS - 1)
            if keep:
                at = jnp.where((local >= 0) & (local < CELLS), at, j)
            back_send[k - 1][d][h][j] = ref[at]

        loop(filled, functools.partial(merge, keep=True), 8)
        loop(width - filled, lambda j: merge(filled + j, False), 8)
        if k > 1:
            landing = back[k - 2][d][h].at[pl.ds(0, width)]
        else:
            landing = back_last[h].at[pl.ds(d * width, width)]
        back_copies[k, d, h] = remote(
            back_send[k - 1][d][h], landing,
            back_ss.at[k - 1, d, h], back_rs.at[k - 1, d, h], toward[1 - d],
        )

    sent = set()

    def ensure_y(delta):
        if delta not in sent:
            sent.add(delta)
            send_y(delta)

    for k in range(hops, 0, -1):
        for d in range(2):
            ensure_y(planes - k if d == 0 else k)
        for delta in (planes - k + 1, k - 1):
            if k == hops and 0 < delta < planes:
                ensure_y(delta)
        for h in range(CHUNKS):
            for d in range(2):
                send_back(k, d, h)
    ensure_y(0)

    end = tab[ENDS + z]
    ups = tab[UPS + z]
    for h in range(CHUNKS):
        for d in range(2):
            back_copies[1, d, h].wait_recv()
        wait_y(0, h)

        def finish(b, h=h):
            rank = tab[RANK_OF + b]
            local = tab[CELL_OF + rank] - z * CELLS
            up = (end - 1 - rank) & (nblk - 1)
            down = (rank - end) & (nblk - 1)
            room = capacity[0]
            at = jnp.where(up < ups, jnp.minimum(up, room - 1), room + jnp.minimum(down, room - 1))
            mine = (local >= 0) & (local < CELLS)
            at = jnp.where(mine, 2 * room + jnp.clip(local, 0, CELLS - 1), at)
            value = back_last[h][at].astype(jnp.float32)
            wide = jnp.concatenate([value[:8], value[8:]], axis=1).astype(jnp.bfloat16)
            column = (b % per_row) * BLK + h * 256
            out[b // per_row, :, pl.ds(pl.multiple_of(column, 256), 256)] = wide

        loop(nblk, finish, 8)

    for copy in sends:
        copy.wait_send()


def ring_call(grad, table, left_root, right_root, planes, capacity):
    row_blocks, piece_rows, width = grad.shape
    nblk = row_blocks * (width // BLK)
    rows = left_root.shape[-1]
    hops = len(capacity)
    tile = (16, 128)
    bf16, f32 = jnp.bfloat16, jnp.float32
    vmem = pltpu.VMEM
    dma = pltpu.SemaphoreType.DMA

    def tiles(*counts):
        return [vmem((count, *tile), bf16) for count in counts for _ in range(CHUNKS)]

    scratch = [
        vmem((SLOTS, rows, rows), bf16),
        vmem((SLOTS, BLK, BLK), bf16),
        vmem((SLOTS, rows, BLK), bf16),
        vmem((SLOTS, rows, BLK), bf16),
        vmem((SLOTS, rows, BLK), f32),
        vmem((SLOTS, 8, 128), f32),
        vmem((SLOTS, *tile), f32),
    ]
    twice = [capacity[k // 2] for k in range(2 * hops)]
    scratch += tiles(nblk)
    scratch += tiles(*twice[:2])
    scratch += tiles(*twice[:-2])
    scratch += tiles(2 * capacity[-1])
    scratch += [vmem((planes, CHUNKS, NX, SLOTS, *tile), bf16) for _ in range(3)]
    scratch += tiles(*twice)
    scratch += tiles(*[count + CELLS for count in twice[2:]])
    scratch += tiles(CELLS)
    scratch += tiles(2 * capacity[0] + CELLS)
    scratch += [dma((2,))]
    scratch += [dma((hops, 2, CHUNKS))] * 2
    scratch += [dma((planes, CHUNKS, NX))] * 4
    scratch += [dma((hops, 2, CHUNKS))] * 2
    body = functools.partial(kernel, planes, nblk, capacity)
    in_vmem = pl.BlockSpec(memory_space=pltpu.VMEM)
    return pl.pallas_call(
        body,
        out_shape=(
            jax.ShapeDtypeStruct(grad.shape, bf16),
            jax.ShapeDtypeStruct((8, 128), f32),
        ),
        in_specs=[
            pl.BlockSpec(memory_space=pltpu.SMEM),
            in_vmem,
            pl.BlockSpec(memory_space=pl.ANY),
            pl.BlockSpec(memory_space=pl.ANY),
        ],
        out_specs=(in_vmem, in_vmem),
        scratch_shapes=scratch,
        compiler_params=pltpu.CompilerParams(
            collective_id=0, has_side_effects=True, vmem_limit_bytes=50 * 1024 * 1024
        ),
        cost_estimate=pl.CostEstimate(
            flops=4 * SLOTS * rows * rows * BLK, bytes_accessed=4 * 1024 * 1024, transcendentals=0
        ),
        name="sorted_ring",
    )(table, grad, left_root, right_root)


def precondition(block, left_factor, right_factor):
    left_part = jnp.dot(left_factor, block, preferred_element_type=jnp.float32).astype(jnp.bfloat16)
    product = jnp.dot(left_part, right_factor, preferred_element_type=jnp.float32)
    grad_mean = jnp.mean(jnp.square(block.astype(jnp.float32)))
    prod_mean = jnp.mean(jnp.square(product))
    update = product * (jnp.sqrt(grad_mean + EPSILON) / jnp.sqrt(prod_mean + EPSILON))
    return (update, jnp.sum(update * update))


def padded_call(grad, cell, left_root, right_root, dp_size):
    row_blocks, piece_rows, width = grad.shape
    col_blocks = width // BLK
    per_group = row_blocks * col_blocks
    position = (cell % SLOTS) * dp_size + cell // SLOTS
    select = (position[None, :] == jnp.arange(SLOTS * dp_size, dtype=jnp.int32)[:, None]).astype(jnp.bfloat16)
    pieces = (
        grad.reshape(row_blocks, piece_rows, col_blocks, BLK)
        .transpose(0, 2, 1, 3)
        .reshape(per_group, piece_rows * BLK)
    )
    outgoing = jnp.dot(select, pieces, preferred_element_type=jnp.float32).astype(jnp.bfloat16)
    outgoing = outgoing.reshape(SLOTS, dp_size * piece_rows, BLK)
    arrived = lax.all_to_all(outgoing, "dp", split_axis=1, concat_axis=1, tiled=True)
    outcomes = [precondition(arrived[s], left_root[0, s], right_root[0, s]) for s in range(SLOTS)]
    updates = jnp.stack([outcome[0] for outcome in outcomes]).astype(jnp.bfloat16)
    partial_sum = sum([outcome[1] for outcome in outcomes])
    returned = lax.all_to_all(updates, "dp", split_axis=1, concat_axis=1, tiled=True)
    placed = jnp.take(returned.reshape(SLOTS * dp_size, piece_rows * BLK), position, axis=0)
    placed = placed.reshape(row_blocks, col_blocks, piece_rows, BLK).transpose(0, 2, 1, 3)
    return placed.reshape(row_blocks, piece_rows, width), partial_sum


def per_device(capacity, grad, owner, left_root, right_root):
    row_blocks, piece_rows, width = grad.shape
    dp_size = lax.axis_size("dp")
    tensors = lax.axis_size("tensor")
    planes = dp_size // NX
    col_blocks = width // BLK
    owners = owner.reshape(row_blocks, tensors, col_blocks).transpose(1, 0, 2).reshape(tensors, -1)
    cell, rank = block_cells(owners)
    ends, ups, fits = plane_split(cell, planes, capacity)
    tables = jax.vmap(functools.partial(make_table, devices=dp_size))(cell, rank, ends, ups)
    tensor_index = lax.axis_index("tensor")
    table = lax.dynamic_index_in_dim(tables, tensor_index, 0, keepdims=False)
    cell_here = lax.dynamic_index_in_dim(cell, tensor_index, 0, keepdims=False)

    def fast(grad, table, cell_here, left_root, right_root):
        moved, squares = ring_call(grad, table, left_root, right_root, planes, capacity)
        return moved, squares[0, 0]

    def padded(grad, table, cell_here, left_root, right_root):
        return padded_call(grad, cell_here, left_root, right_root, dp_size)

    moved, squares = lax.cond(fits, fast, padded, grad, table, cell_here, left_root, right_root)
    squares = lax.psum(squares, ("dp", "tensor"))
    cells = row_blocks * piece_rows * dp_size * width * tensors
    update_rms = jnp.sqrt(squares / cells + EPSILON)
    direction = (moved.astype(jnp.float32) * (1.0 / update_rms)).astype(jnp.bfloat16)
    return (direction, update_rms)


def build(mesh, capacity):
    return jax.shard_map(
        functools.partial(per_device, capacity),
        mesh=mesh,
        in_specs=(
            P(None, "dp", "tensor"),
            P(),
            P("tensor", "dp", None, None),
            P("tensor", "dp", None, None),
        ),
        out_specs=(P(None, "dp", "tensor"), P()),
        check_vma=False,
    )


def solution(mesh):
    return build(mesh, CAPACITY)
```

time: 369 us -> 234 us (0.63); the launches traced: 363 us -> 234 us
  Pallas kernels: 0 us -> 110 us
  blocking collectives: 219 us -> 112 us
  waiting for transfers between devices: 94.6 us -> 0 us
  local copies, waits for them, and re-layouts: 14.5 us -> 1.56 us
  matrix products: 10.9 us -> 0 us
  starting transfers between devices: 7.94 us -> 0 us
  between operations: 8.51 us -> 3.22 us
    all_to_all x1 -> x0, blocking collectives: 114 us -> none  [per_device(): lax.all_to_all(outgoing, 'dp', split_axis=1, concat_axis=1, tiled=True)]
    pallas_call x0 -> x1, Pallas kernels: none -> 110 us  [ring_call(): pl.pallas_call(body, out_shape=(jax.ShapeDtypeStruct(grad.shape, bf16), j...]
    all_to_all x1 -> x0, waiting for transfers between devices: 94.6 us -> none  [per_device(): lax.all_to_all((updates * inv_rms).astype(jnp.bfloat16), 'dp', split_axis...]
    dot_general x4 -> x0, matrix products: 10.9 us -> none  [the longest x3 10.4 us: precondition(): jnp.dot(left_part, right_factor, preferred_element_type=jnp.float32)]
    all_to_all x1 -> x0, starting transfers between devices: 7.94 us -> none  [per_device(): lax.all_to_all((updates * inv_rms).astype(jnp.bfloat16), 'dp', split_axis...]
    psum x1, blocking collectives: 106 us -> 112 us  [per_device(): squares = lax.psum(squares, ('dp', 'tensor'))]
    reshape x4 -> x1, local copies, waits for them, and re-layouts: 4.8 us -> 0.06 us  [per_device(): owner.reshape(row_blocks, tensors, col_blocks).transpose(1, 0, 2)]
  transfers between devices with their start and end apart: 1 -> 0, of which waited for: 1 -> 0; matrix products, arithmetic and copies ran while one was open for 0% -> 0% of each run, Pallas kernels for 0% -> 0%
where the time goes in v1:
time: 234 us
  blocking collectives  112 us (48%)
  Pallas kernels  110 us (47%)
  other arithmetic  6.88 us (3%)
  between operations  3.22 us (1%)
    psum x1, blocking collectives, per_device(): squares = lax.psum(squares, ('dp', 'tensor'))  112 us
    pallas_call x1, Pallas kernels, ring_call(): pl.pallas_call(body, out_shape=(jax.ShapeDtypeStruct(grad.shape, bf16), j...  110 us

profile of v1, /device:TPU:1, one launch (start us, length us, event | category | flops | bytes accessed | tf_op | source)
XLA Modules:
  0.0 234.0 jit_solution(1746217718483415816)
XLA Ops:
  0.6 0.8 copy.53
  1.4 0.1 copy.54
  1.5 0.1 copy.55
  1.6 0.3 convert_reduce_fusion.3
  1.9 0.2 convert_reduce_fusion.4
  2.1 2.4 %convert_reduce_fusion = s32[8,16,17]{1,2,0:T(8,128)S(1)} fusion(s32[8,16,64]{2,1,0:T(8,128)S(1)} %get-tuple-element.115), kind=kLoop, calls=%fused_computation.69 | loop fusion | flops 415616 | bytes 41472 | tf_op jit(solution)/shard_map/reduce_sum | solution.py:38
  4.5 0.8 fusion.37
  5.3 0.8 add_reduce_fusion
  6.1 0.3 convert_reduce_fusion.2
  6.4 0.3 select_reduce_fusion
  6.8 0.2 convert_reduce_fusion.1
  6.9 0.1 concatenate.3
  7.0 0.6 compare_reduce_fusion
  8.3 111.2 %conditional.3 = (f32[]{:T(128)}, f32[16,8,2048]{2,1,0:T(8,128)S(1)}) conditional(s32[]{:T(128)} %convert_element_type.59, (s32[8,64]{0,1:T(8,128)S(1)}, s32[8,64]{1,0:T(8,128)S(1)}, s32[]{:T(128)}, bf16[16,8,2048]{2,1,0:T(8,128)(2,1)}, bf16[1,3,512,512]{3,2,1,0:T(8,128)(2,1)}, /*index=5*/bf16[1,3,512,512]{3,2,1,0:T(8,128)(2,1)}) %tuple.54, ...), branch_computations={%region_10.20_spmd, %region_20.21_spmd} | conditional | flops 1722041344 | bytes 51924972
  8.6 109.7 %sorted_ring.1 = (bf16[16,8,2048]{2,1,0:T(8,128)(2,1)S(1)}, f32[8,128]{1,0:T(8,128)S(1)}) custom-call(s32[416]{0:T(512)S(1)} %bitcast.115, bf16[16,8,2048]{2,1,0:T(8,128)(2,1)} %get-tuple-element.48.refs_1_, bf16[1,3,512,512]{3,2,1,0:T(8,128)(2,1)} %get-tuple-element.49.refs_2_, bf16[1,3,512,512]{3,2,1,0:T(8,128)(2,1)} %get-tuple-element.50.refs_3_), custom_call_target="tpu_custom_call" | custom-call | flops 1610612736 | bytes 4194304 | tf_op jit(solution)/shard_map/cond/branch_1_fun/sorted_ring/pallas_call | solution.py:443
  118.2 0.1 convert_element_type.66
  118.3 0.5 slice.35
  119.5 111.8 %psum.7 = f32[]{:T(128)} all-reduce(f32[]{:T(128)} %get-tuple-element.58), channel_id=1, replica_groups=mesh['dp'=64,'tensor'=8] {'dp','tensor'}, use_global_device_ids=true, to_apply=%region_21.22 | all-reduce | flops 1 | bytes 8 | tf_op jit(solution)/shard_map/psum | solution.py:521
  232.0 0.9 multiply_convert_fusion.3
  (6 shorter events, 0.1 us)

commit v2 on v1

--- a/solution.py
+++ b/solution.py
@@ -85,7 +85,7 @@
         return [take(*shape[1:]) for _ in range(shape[0])]
 
     tab, grad, left_hbm, right_hbm = take(4)
-    out, ssq_out = take(2)
+    out, rms_out = take(2)
     left, right, mats, halves, prods, scales, squares = take(7)
     folded = take(CHUNKS)
     first = take(2, CHUNKS)
@@ -96,11 +96,13 @@
     back = take(hops - 1, 2, CHUNKS)
     back_first = take(CHUNKS)
     back_last = take(CHUNKS)
-    load_sem, ring_ss, ring_rs, x_ss, x_rs, y_ss, y_rs, back_ss, back_rs = take(9)
+    sums = take()
+    load_sem, ring_ss, ring_rs, x_ss, x_rs, y_ss, y_rs, back_ss, back_rs, sum_ss, sum_rs = take(11)
 
     rows = mats.shape[1]
     dp = lax.axis_index("dp")
     tensor = lax.axis_index("tensor")
+    tensors = lax.axis_size("tensor")
     z, x = dp // NX, dp % NX
     devices = planes * NX
     per_row = nblk // grad.shape[0]
@@ -125,7 +127,16 @@
         copy.start()
 
     barrier = pltpu.get_barrier_semaphore()
-    peers = toward + along[1:]
+    partners = []
+    stride = 1
+    while stride < tensors:
+        partners.append((dp, tensor + stride - 2 * stride * ((tensor // stride) % 2)))
+        stride *= 2
+    stride = 1
+    while stride < devices:
+        partners.append((dp + stride - 2 * stride * ((dp // stride) % 2), tensor))
+        stride *= 2
+    peers = toward + along[1:] + partners
     for peer in peers:
         pl.semaphore_signal(barrier, inc=1, device_id=peer, device_id_type=MESH)
 
@@ -284,7 +295,20 @@
         return total + jnp.where(held, prod_sum * scale * scale, 0.0)
 
     total = lax.fori_loop(0, SLOTS, right_part, jnp.zeros((1, 1), jnp.float32))
-    ssq_out[...] = jnp.broadcast_to(total, ssq_out.shape)
+    stages = len(partners)
+    sums[0] = jnp.broadcast_to(total, sums.shape[1:])
+    sum_copies = []
+
+    def exchange():
+        i = len(sum_copies)
+        if i:
+            sum_copies[i - 1].wait_recv()
+            sums[2 * i] = sums[2 * i - 2] + sums[2 * i - 1]
+        if i < stages:
+            sum_copies.append(
+                remote(sums.at[2 * i], sums.at[2 * i + 1], sum_ss.at[i], sum_rs.at[i], partners[i])
+            )
+
 
     y_copies = {}
 
@@ -373,7 +397,15 @@
         for h in range(CHUNKS):
             for d in range(2):
                 send_back(k, d, h)
+            if len(sum_copies) < stages:
+                exchange()
     ensure_y(0)
+    while len(sum_copies) < stages:
+        exchange()
+    exchange()
+    update_rms = jnp.sqrt(sums[2 * stages] / (nblk * cells * tensors) + EPSILON)
+    rms_out[...] = update_rms
+    inv_rms = (1.0 / update_rms)[:1, :1]
 
     end = tab[ENDS + z]
     ups = tab[UPS + z]
@@ -391,7 +423,7 @@
             at = jnp.where(up < ups, jnp.minimum(up, room - 1), room + jnp.minimum(down, room - 1))
             mine = (local >= 0) & (local < CELLS)
             at = jnp.where(mine, 2 * room + jnp.clip(local, 0, CELLS - 1), at)
-            value = back_last[h][at].astype(jnp.float32)
+            value = back_last[h][at].astype(jnp.float32) * inv_rms
             wide = jnp.concatenate([value[:8], value[8:]], axis=1).astype(jnp.bfloat16)
             column = (b % per_row) * BLK + h * 256
             out[b // per_row, :, pl.ds(pl.multiple_of(column, 256), 256)] = wide
@@ -402,7 +434,7 @@
         copy.wait_send()
 
 
-def ring_call(grad, table, left_root, right_root, planes, capacity):
+def ring_call(grad, table, left_root, right_root, planes, tensors, capacity):
     row_blocks, piece_rows, width = grad.shape
     nblk = row_blocks * (width // BLK)
     rows = left_root.shape[-1]
@@ -434,10 +466,13 @@
     scratch += tiles(*[count + CELLS for count in twice[2:]])
     scratch += tiles(CELLS)
     scratch += tiles(2 * capacity[0] + CELLS)
+    stages = (planes * NX * tensors).bit_length() - 1
+    scratch += [vmem((2 * stages + 1, 8, 128), f32)]
     scratch += [dma((2,))]
     scratch += [dma((hops, 2, CHUNKS))] * 2
     scratch += [dma((planes, CHUNKS, NX))] * 4
     scratch += [dma((hops, 2, CHUNKS))] * 2
+    scratch += [dma((stages,))] * 2
     body = functools.partial(kernel, planes, nblk, capacity)
     in_vmem = pl.BlockSpec(memory_space=pltpu.VMEM)
     return pl.pallas_call(
@@ -493,7 +528,10 @@
     returned = lax.all_to_all(updates, "dp", split_axis=1, concat_axis=1, tiled=True)
     placed = jnp.take(returned.reshape(SLOTS * dp_size, piece_rows * BLK), position, axis=0)
     placed = placed.reshape(row_blocks, col_blocks, piece_rows, BLK).transpose(0, 2, 1, 3)
-    return placed.reshape(row_blocks, piece_rows, width), partial_sum
+    cells = per_group * dp_size * piece_rows * BLK * lax.axis_size("tensor")
+    update_rms = jnp.sqrt(lax.psum(partial_sum, ("dp", "tensor")) / cells + EPSILON)
+    direction = placed.reshape(row_blocks, piece_rows, width).astype(jnp.float32) * (1.0 / update_rms)
+    return direction.astype(jnp.bfloat16), update_rms
 
 
 def per_device(capacity, grad, owner, left_root, right_root):
@@ -511,18 +549,13 @@
     cell_here = lax.dynamic_index_in_dim(cell, tensor_index, 0, keepdims=False)
 
     def fast(grad, table, cell_here, left_root, right_root):
-        moved, squares = ring_call(grad, table, left_root, right_root, planes, capacity)
-        return moved, squares[0, 0]
+        moved, rms = ring_call(grad, table, left_root, right_root, planes, tensors, capacity)
+        return moved, rms[0, 0]
 
     def padded(grad, table, cell_here, left_root, right_root):
         return padded_call(grad, cell_here, left_root, right_root, dp_size)
 
-    moved, squares = lax.cond(fits, fast, padded, grad, table, cell_here, left_root, right_root)
-    squares = lax.psum(squares, ("dp", "tensor"))
-    cells = row_blocks * piece_rows * dp_size * width * tensors
-    update_rms = jnp.sqrt(squares / cells + EPSILON)
-    direction = (moved.astype(jnp.float32) * (1.0 / update_rms)).astype(jnp.bfloat16)
-    return (direction, update_rms)
+    return lax.cond(fits, fast, padded, grad, table, cell_here, left_root, right_root)
 
 
 def build(mesh, capacity):

time: 234 us -> 143 us (0.61)
  the two profiles are of different devices: /device:TPU:1 before, /device:TPU:32 now
where the time goes in v2:
time: 143 us
  Pallas kernels  131 us (92%)
  other arithmetic  5.91 us (4%)
  between operations  2.49 us (2%)
  local copies, waits for them, and re-layouts  2.35 us (2%)
    pallas_call x1, Pallas kernels, ring_call(): pl.pallas_call(body, out_shape=(jax.ShapeDtypeStruct(grad.shape, bf16), j...  131 us

profile of v2, /device:TPU:32, one launch (start us, length us, event | category | flops | bytes accessed | tf_op | source)
XLA Modules:
  0.0 143.1 jit_solution(13953663564449832789)
XLA Ops:
  0.6 0.8 copy.55
  1.4 0.1 copy.56
  1.5 0.1 copy.57
  1.6 0.3 convert_reduce_fusion.3
  1.9 0.2 convert_reduce_fusion.4
  2.1 2.4 %convert_reduce_fusion = s32[8,16,17]{1,2,0:T(8,128)S(1)} fusion(s32[8,16,64]{2,1,0:T(8,128)S(1)} %get-tuple-element.103), kind=kLoop, calls=%fused_computation.69 | loop fusion | flops 415616 | bytes 41472 | tf_op jit(solution)/shard_map/reduce_sum | solution.py:38
  4.5 0.8 fusion.37
  5.3 0.8 add_reduce_fusion
  6.1 0.3 convert_reduce_fusion.2
  6.4 0.3 select_reduce_fusion
  6.8 0.2 convert_reduce_fusion.1
  6.9 0.1 concatenate.3
  7.0 0.6 compare_reduce_fusion
  8.3 132.8 %conditional.1 = (f32[]{:T(128)}, bf16[16,8,2048]{2,1,0:T(8,128)(2,1)S(1)}) conditional(s32[]{:T(128)} %convert_element_type.61, (s32[8,64]{0,1:T(8,128)S(1)}, s32[8,64]{1,0:T(8,128)S(1)}, s32[]{:T(128)}, bf16[16,8,2048]{2,1,0:T(8,128)(2,1)}, bf16[1,3,512,512]{3,2,1,0:T(8,128)(2,1)}, /*index=5*/bf16[1,3,512,512]{3,2,1,0:T(8,128)(2,1)}) %tuple.44, ...), branch_computations={%region_10.21_spmd, %region_21.22_spmd} | conditional | flops 1722565632 | bytes 51400740 | solution.py:558
  8.6 131.4 %sorted_ring.1 = (bf16[16,8,2048]{2,1,0:T(8,128)(2,1)S(1)}, f32[8,128]{1,0:T(8,128)S(1)}) custom-call(s32[416]{0:T(512)S(1)} %bitcast.115, bf16[16,8,2048]{2,1,0:T(8,128)(2,1)} %get-tuple-element.40.refs_1_, bf16[1,3,512,512]{3,2,1,0:T(8,128)(2,1)} %get-tuple-element.41.refs_2_, bf16[1,3,512,512]{3,2,1,0:T(8,128)(2,1)} %get-tuple-element.42.refs_3_), custom_call_target="tpu_custom_call" | custom-call | flops 1610612736 | bytes 4194304 | tf_op jit(solution)/shard_map/cond/branch_1_fun/sorted_ring/pallas_call | solution.py:478
  140.0 0.5 slice.35
  141.1 0.8 copy.92
  (6 shorter events, 0.1 us)

commit v3 on v2

--- a/solution.py
+++ b/solution.py
@@ -15,35 +15,39 @@
 SLOTS = 3
 CELLS = NX * SLOTS
 CHUNKS = 2
-CAPACITY = (43, 38, 35, 29, 25, 20, 13, 8)
+BITS = (1, 2, 4, 8, 16, 32)
+DISTANCE = ((0, 1, 2, 0, 0, 0), (1, 2, 1, 2, 4, 8))
+CAPACITY = (42, 37, 34, 28, 24, 19, 12, 7)
 
 
 def block_cells(owners):
-    n = owners.shape[-1]
+    n = owners.shape[0]
     index = jnp.arange(n, dtype=jnp.int32)
-    same = owners[:, :, None] == owners[:, None, :]
-    slot = jnp.sum((same & (index[None, :] < index[:, None])).astype(jnp.int32), axis=-1)
+    same = owners[:, None] == owners[None, :]
+    slot = jnp.sum((same & (index[None, :] < index[:, None])).astype(jnp.int32), axis=1)
     cell = owners * SLOTS + slot
-    rank = jnp.sum((cell[:, None, :] < cell[:, :, None]).astype(jnp.int32), axis=-1)
+    rank = jnp.sum((cell[None, :] < cell[:, None]).astype(jnp.int32), axis=1)
     return cell, rank
 
 
-def plane_split(cell, planes, capacity):
-    n = cell.shape[-1]
+def plane_split(owner, tensors, planes, capacity):
     hops = len(capacity)
-    planes_of = cell // CELLS
     z = jnp.arange(planes, dtype=jnp.int32)
-    distance = (planes_of[:, None, :] - z[None, :, None]) % planes
-    steps = jnp.arange(planes + 1, dtype=jnp.int32)
-    nearer = jnp.sum((distance[:, :, None, :] < steps[None, None, :, None]).astype(jnp.int32), axis=-1)
-    room = jnp.array(tuple(capacity) + (0,), jnp.int32)
-    up_limit = jnp.min(nearer[:, :, 1 : hops + 2] + room, axis=-1)
-    down_limit = jnp.max(nearer[:, :, planes - hops : planes + 1][:, :, ::-1] - room, axis=-1)
-    local = nearer[:, :, 1]
-    fits = jnp.all(down_limit <= up_limit)
-    cut = jnp.clip((down_limit + up_limit) // 2, local, n)
-    starts = jnp.sum((planes_of[:, None, :] < z[None, :, None]).astype(jnp.int32), axis=-1)
-    return starts + cut, cut - local, fits
+    counts = jnp.sum((owner[:, :, None] // NX == z).astype(jnp.float32), axis=0)
+    counts = jnp.sum(counts.reshape(tensors, -1, planes), axis=1)
+    q = jnp.arange(2 * planes + 1, dtype=jnp.int32)
+    turns = (z[:, None] < q[None, :]).astype(jnp.float32) + (z[:, None] + planes < q[None, :]).astype(jnp.float32)
+    below = jnp.dot(counts, turns, precision=lax.Precision.HIGHEST).astype(jnp.int32)
+    room = tuple(capacity) + (0,)
+    high, low = None, None
+    for k in range(1, hops + 2):
+        up = below[:, k : k + planes] + room[k - 1]
+        down = below[:, planes + 1 - k : 2 * planes + 1 - k] - room[k - 1]
+        high = up if high is None else jnp.minimum(high, up)
+        low = down if low is None else jnp.maximum(low, down)
+    first = below[:, 1 : planes + 1]
+    ends = jnp.maximum((high + low) // 2, first)
+    return ends, ends - first, jnp.all(low <= high)
 
 
 def make_table(cell, rank, ends, ups, devices):
@@ -128,45 +132,48 @@
 
     barrier = pltpu.get_barrier_semaphore()
     partners = []
-    stride = 1
-    while stride < tensors:
-        partners.append((dp, tensor + stride - 2 * stride * ((tensor // stride) % 2)))
-        stride *= 2
-    stride = 1
-    while stride < devices:
-        partners.append((dp + stride - 2 * stride * ((dp // stride) % 2), tensor))
-        stride *= 2
-    peers = toward + along[1:] + partners
+    bits = [(stride, place) for place, size in ((0, tensors), (1, devices)) for stride in BITS if stride < size]
+    for stride, place in sorted(bits, key=lambda bit: (DISTANCE[bit[1]][BITS.index(bit[0])], bit)):
+        if place:
+            partners.append((dp + stride - 2 * stride * ((dp // stride) % 2), tensor))
+        else:
+            partners.append((dp, tensor + stride - 2 * stride * ((tensor // stride) % 2)))
+    peers = toward + along[1:] + [partner for partner in partners if partner[0] is dp]
     for peer in peers:
         pl.semaphore_signal(barrier, inc=1, device_id=peer, device_id_type=MESH)
 
-    def fold_row(r):
-        for c in range(per_row):
-            piece = grad[r, :, pl.ds(c * BLK, BLK)].astype(jnp.float32)
-            for h in range(CHUNKS):
-                folded[h][r * per_row + c] = fold(piece[:, h * 256 : (h + 1) * 256])
-
-    loop(grad.shape[0], fold_row, 2)
-
     end = tab[ENDS + z]
 
-    def fill_first(j):
-        for d, r in ((0, (end - 1 - j) & (nblk - 1)), (1, (end + j) & (nblk - 1))):
-            block = tab[r]
-            for h in range(CHUNKS):
-                first[d][h][j] = folded[h][block]
-
-    loop(capacity[0], fill_first, 4)
-
+    def fill_chunk(h):
+        def fold_row(r):
+            for c in range(per_row):
+                piece = grad[r, :, pl.ds(c * BLK + h * 256, 256)].astype(jnp.float32)
+                folded[h][r * per_row + c] = fold(piece)
+
+        def fill_first(j):
+            first[0][h][j] = folded[h][tab[(end - 1 - j) & (nblk - 1)]]
+            first[1][h][j] = folded[h][tab[(end + j) & (nblk - 1)]]
+
+        loop(grad.shape[0], fold_row, 4)
+        loop(capacity[0], fill_first, 8)
+
+    fill_chunk(0)
     pl.semaphore_wait(barrier, len(peers))
 
     sends = []
 
-    def remote(src, dst, ss, rs, target):
-        copy = pltpu.make_async_remote_copy(
+    def describe(src, dst, ss, rs, target):
+        return pltpu.make_async_remote_copy(
             src_ref=src, dst_ref=dst, send_sem=ss, recv_sem=rs, device_id=target, device_id_type=MESH
         )
+
+    def start(*args):
+        copy = describe(*args)
         copy.start()
+        return copy
+
+    def remote(*args):
+        copy = start(*args)
         sends.append(copy)
         return copy
 
@@ -184,22 +191,20 @@
         )
 
     for h in range(CHUNKS):
+        if h:
+            fill_chunk(h)
         for d in range(2):
             send_ring(1, d, h)
 
-    x_copies = {}
-
     def send_x(delta, h):
-        x_copies[delta, h] = [
-            remote(xs.at[delta, h, rel], xr.at[delta, h, rel], x_ss.at[delta, h, rel], x_rs.at[delta, h, rel], along[rel])
-            for rel in range(1, NX)
-        ]
+        for rel in range(1, NX):
+            start(xs.at[delta, h, rel - 1], xr.at[delta, h, rel], x_ss.at[0], x_rs.at[delta, h], along[rel])
 
     def put_x(delta, h, rel, s, value):
         if rel == 0:
             xr[delta, h, 0, s] = value
         else:
-            xs[delta, h, rel, s] = value
+            xs[delta, h, rel - 1, s] = value
 
     def cell_index(rel, s):
         return z * CELLS + ((x + rel) % NX) * SLOTS + s
@@ -236,8 +241,8 @@
     squares[...] = jnp.zeros_like(squares)
 
     def place(delta, h):
-        for copy in x_copies[delta, h]:
-            copy.wait_recv()
+        arrived = xr.at[delta, h, pl.ds(1, NX - 1)]
+        describe(arrived, arrived, x_ss.at[0], x_rs.at[delta, h], along[1]).wait_recv()
         source = plane(-delta)
         for s in range(SLOTS):
             total = None
@@ -310,8 +315,6 @@
             )
 
 
-    y_copies = {}
-
     def y_at(delta, h):
         if delta == 0:
             return back_last[h], 2 * capacity[0]
@@ -333,20 +336,20 @@
                         ref, row = y_at(delta, h)
                         ref[row + x * SLOTS + s] = part
                     else:
-                        ys[delta, h, rel, s] = part
+                        ys[delta, h, rel - 1, s] = part
         for h in range(CHUNKS):
             ref, row = y_at(delta, h)
-            y_copies[delta, h] = [
-                remote(
-                    ys.at[delta, h, rel], ref.at[pl.ds(row + x * SLOTS, SLOTS)],
-                    y_ss.at[delta, h, rel], y_rs.at[delta, h, rel], along[rel],
-                )
-                for rel in range(1, NX)
-            ]
+            for rel in range(1, NX):
+                landing = ref.at[pl.ds(row + x * SLOTS, SLOTS)]
+                start(ys.at[delta, h, rel - 1], landing, y_ss.at[0], y_rs.at[delta, h], along[rel])
+
+    waited = set()
 
     def wait_y(delta, h):
-        for copy in y_copies.pop((delta, h), ()):
-            copy.wait_recv()
+        if (delta, h) not in waited:
+            waited.add((delta, h))
+            alike = ys.at[delta, h]
+            describe(alike, alike, y_ss.at[0], y_rs.at[delta, h], along[1]).wait_recv()
 
     back_copies = {}
 
@@ -381,6 +384,8 @@
             back_ss.at[k - 1, d, h], back_rs.at[k - 1, d, h], toward[1 - d],
         )
 
+    points = [(k, h) for k in range(hops - 2, 1, -1) for h in range(CHUNKS)]
+    points = (points[:-2] + points[-1:])[:stages]
     sent = set()
 
     def ensure_y(delta):
@@ -389,22 +394,20 @@
             send_y(delta)
 
     for k in range(hops, 0, -1):
-        for d in range(2):
-            ensure_y(planes - k if d == 0 else k)
-        for delta in (planes - k + 1, k - 1):
-            if k == hops and 0 < delta < planes:
-                ensure_y(delta)
+        for ahead in range(k, max(k - 3, -1), -1):
+            ensure_y((planes - ahead) % planes)
+            ensure_y(ahead)
         for h in range(CHUNKS):
             for d in range(2):
                 send_back(k, d, h)
-            if len(sum_copies) < stages:
+            if (k, h) in points:
                 exchange()
     ensure_y(0)
     while len(sum_copies) < stages:
         exchange()
     exchange()
     update_rms = jnp.sqrt(sums[2 * stages] / (nblk * cells * tensors) + EPSILON)
-    rms_out[...] = update_rms
+    rms_out[0, 0] = update_rms[0, 0]
     inv_rms = (1.0 / update_rms)[:1, :1]
 
     end = tab[ENDS + z]
@@ -432,6 +435,8 @@
 
     for copy in sends:
         copy.wait_send()
+    describe(xs, xs, x_ss.at[0], x_rs.at[0, 0], along[1]).wait_send()
+    describe(ys, ys, y_ss.at[0], y_rs.at[0, 0], along[1]).wait_send()
 
 
 def ring_call(grad, table, left_root, right_root, planes, tensors, capacity):
@@ -461,7 +466,7 @@
     scratch += tiles(*twice[:2])
     scratch += tiles(*twice[:-2])
     scratch += tiles(2 * capacity[-1])
-    scratch += [vmem((planes, CHUNKS, NX, SLOTS, *tile), bf16) for _ in range(3)]
+    scratch += [vmem((planes, CHUNKS, n, SLOTS, *tile), bf16) for n in (NX - 1, NX, NX - 1)]
     scratch += tiles(*twice)
     scratch += tiles(*[count + CELLS for count in twice[2:]])
     scratch += tiles(CELLS)
@@ -470,7 +475,7 @@
     scratch += [vmem((2 * stages + 1, 8, 128), f32)]
     scratch += [dma((2,))]
     scratch += [dma((hops, 2, CHUNKS))] * 2
-    scratch += [dma((planes, CHUNKS, NX))] * 4
+    scratch += [dma((1,)), dma((planes, CHUNKS))] * 2
     scratch += [dma((hops, 2, CHUNKS))] * 2
     scratch += [dma((stages,))] * 2
     body = functools.partial(kernel, planes, nblk, capacity)
@@ -479,7 +484,7 @@
         body,
         out_shape=(
             jax.ShapeDtypeStruct(grad.shape, bf16),
-            jax.ShapeDtypeStruct((8, 128), f32),
+            jax.ShapeDtypeStruct((1, 1), f32),
         ),
         in_specs=[
             pl.BlockSpec(memory_space=pltpu.SMEM),
@@ -487,7 +492,7 @@
             pl.BlockSpec(memory_space=pl.ANY),
             pl.BlockSpec(memory_space=pl.ANY),
         ],
-        out_specs=(in_vmem, in_vmem),
+        out_specs=(in_vmem, pl.BlockSpec(memory_space=pltpu.SMEM)),
         scratch_shapes=scratch,
         compiler_params=pltpu.CompilerParams(
             collective_id=0, has_side_effects=True, vmem_limit_bytes=50 * 1024 * 1024
@@ -540,22 +545,22 @@
     tensors = lax.axis_size("tensor")
     planes = dp_size // NX
     col_blocks = width // BLK
-    owners = owner.reshape(row_blocks, tensors, col_blocks).transpose(1, 0, 2).reshape(tensors, -1)
-    cell, rank = block_cells(owners)
-    ends, ups, fits = plane_split(cell, planes, capacity)
-    tables = jax.vmap(functools.partial(make_table, devices=dp_size))(cell, rank, ends, ups)
     tensor_index = lax.axis_index("tensor")
-    table = lax.dynamic_index_in_dim(tables, tensor_index, 0, keepdims=False)
-    cell_here = lax.dynamic_index_in_dim(cell, tensor_index, 0, keepdims=False)
-
-    def fast(grad, table, cell_here, left_root, right_root):
+    here = lax.dynamic_slice_in_dim(owner, tensor_index * col_blocks, col_blocks, 1).reshape(-1)
+    ends, ups, fits = plane_split(owner, tensors, planes, capacity)
+    cell, rank = block_cells(here)
+    ends = lax.dynamic_index_in_dim(ends, tensor_index, 0, keepdims=False)
+    ups = lax.dynamic_index_in_dim(ups, tensor_index, 0, keepdims=False)
+    table = make_table(cell, rank, ends, ups, dp_size)
+
+    def fast(grad, table, cell, left_root, right_root):
         moved, rms = ring_call(grad, table, left_root, right_root, planes, tensors, capacity)
-        return moved, rms[0, 0]
-
-    def padded(grad, table, cell_here, left_root, right_root):
-        return padded_call(grad, cell_here, left_root, right_root, dp_size)
-
-    return lax.cond(fits, fast, padded, grad, table, cell_here, left_root, right_root)
+        return moved, rms.reshape(())
+
+    def padded(grad, table, cell, left_root, right_root):
+        return padded_call(grad, cell, left_root, right_root, dp_size)
+
+    return lax.cond(fits, fast, padded, grad, table, cell, left_root, right_root)
 
 
 def build(mesh, capacity):

time: 143 us -> 120 us (0.84)
  the two profiles are of different devices: /device:TPU:32 before, /device:TPU:1 now
where the time goes in v3:
time: 120 us; the launch traced here: 117 us
  Pallas kernels  110 us (92%)
  between operations  2.48 us (2%)
  other arithmetic  2.08 us (2%)
  local copies, waits for them, and re-layouts  1.83 us (2%)
    pallas_call x1, Pallas kernels, ring_call(): pl.pallas_call(body, out_shape=(jax.ShapeDtypeStruct(grad.shape, bf16), j...  110 us

profile of v3, /device:TPU:1, one launch (start us, length us, event | category | flops | bytes accessed | tf_op | source)
XLA Modules:
  0.0 117.3 jit_solution(3420171561343671055)
XLA Ops:
  0.6 0.8 constant_dynamic-slice_fusion.2
  1.4 0.1 reshape.87
  1.5 0.2 convert_reduce_fusion.3
  1.7 0.2 convert_reduce_fusion.2
  1.9 0.1 select_reduce_fusion
  2.0 0.1 convert_reduce_fusion.1
  2.1 0.7 add_select_fusion
  2.8 0.1 copy.30
  2.9 0.2 convolution_convert_fusion.4
  3.1 0.1 slice_subtract_fusion
  3.3 0.1 concatenate.3
  3.4 0.6 compare_reduce_fusion
  4.6 110.7 %conditional.1 = (f32[]{:T(128)}, bf16[16,8,2048]{2,1,0:T(8,128)(2,1)S(1)}) conditional(s32[]{:T(128)} %convert_element_type.69, (s32[64]{0:T(128)S(1)}, s32[64]{0:T(128)S(1)}, bf16[16,8,2048]{2,1,0:T(8,128)(2,1)}, bf16[1,3,512,512]{3,2,1,0:T(8,128)(2,1)}, bf16[1,3,512,512]{3,2,1,0:T(8,128)(2,1)}) %tuple.15, (s32[416]{0:T(512)S(1)}, ...), branch_computations={%region_8.19_spmd, %region_19.20_spmd} | conditional | flops 1722563072 | bytes 51387028 | solution.py:563
  4.8 109.9 %sorted_ring.1 = (bf16[16,8,2048]{2,1,0:T(8,128)(2,1)S(1)}, f32[1,1]{1,0:T(1,128)}) custom-call(s32[416]{0:T(512)S(1)} %get-tuple-element.27.refs_0_, bf16[16,8,2048]{2,1,0:T(8,128)(2,1)} %get-tuple-element.28.refs_1_, bf16[1,3,512,512]{3,2,1,0:T(8,128)(2,1)} %get-tuple-element.29.refs_2_, bf16[1,3,512,512]{3,2,1,0:T(8,128)(2,1)} %get-tuple-element.30.refs_3_), custom_call_target="tpu_custom_call" | custom-call | flops 1610612736 | bytes 4194304 | tf_op jit(solution)/shard_map/cond/branch_1_fun/sorted_ring/pallas_call | solution.py:483
  115.3 0.8 copy.65
  (5 shorter events, 0.1 us)

commit v4 on v3

--- a/solution.py
+++ b/solution.py
@@ -17,7 +17,7 @@
 CHUNKS = 2
 BITS = (1, 2, 4, 8, 16, 32)
 DISTANCE = ((0, 1, 2, 0, 0, 0), (1, 2, 1, 2, 4, 8))
-CAPACITY = (42, 37, 34, 28, 24, 19, 12, 7)
+CAPACITIES = ((38, 34, 30, 25, 20, 15, 10, 5), (42, 37, 34, 28, 24, 19, 12, 7))
 
 
 def block_cells(owners):
@@ -30,24 +30,27 @@
     return cell, rank
 
 
-def plane_split(owner, tensors, planes, capacity):
-    hops = len(capacity)
+def plane_split(owner, tensors, planes, capacities):
     z = jnp.arange(planes, dtype=jnp.int32)
     counts = jnp.sum((owner[:, :, None] // NX == z).astype(jnp.float32), axis=0)
     counts = jnp.sum(counts.reshape(tensors, -1, planes), axis=1)
     q = jnp.arange(2 * planes + 1, dtype=jnp.int32)
     turns = (z[:, None] < q[None, :]).astype(jnp.float32) + (z[:, None] + planes < q[None, :]).astype(jnp.float32)
     below = jnp.dot(counts, turns, precision=lax.Precision.HIGHEST).astype(jnp.int32)
-    room = tuple(capacity) + (0,)
-    high, low = None, None
-    for k in range(1, hops + 2):
-        up = below[:, k : k + planes] + room[k - 1]
-        down = below[:, planes + 1 - k : 2 * planes + 1 - k] - room[k - 1]
-        high = up if high is None else jnp.minimum(high, up)
-        low = down if low is None else jnp.maximum(low, down)
     first = below[:, 1 : planes + 1]
-    ends = jnp.maximum((high + low) // 2, first)
-    return ends, ends - first, jnp.all(low <= high)
+    level = jnp.full_like(first, len(capacities))
+    ends = first
+    for i, capacity in reversed(list(enumerate(capacities))):
+        high, low = None, None
+        for k, room in enumerate(tuple(capacity) + (0,), 1):
+            up = below[:, k : k + planes] + room
+            down = below[:, planes + 1 - k : 2 * planes + 1 - k] - room
+            high = up if high is None else jnp.minimum(high, up)
+            low = down if low is None else jnp.maximum(low, down)
+        fits = low <= high
+        level = jnp.where(fits, i, level)
+        ends = jnp.where(fits, jnp.maximum((high + low) // 2, first), ends)
+    return ends, ends - first, jnp.max(level)
 
 
 def make_table(cell, rank, ends, ups, devices):
@@ -79,8 +82,13 @@
         body(j)
 
 
+def arrived_slots(capacity):
+    return capacity[1:-2] + (capacity[-2] + capacity[-1], 0)
+
+
 def kernel(planes, nblk, capacity, *refs):
     hops = len(capacity)
+    arrivals = arrived_slots(capacity)
     names = iter(refs)
 
     def take(*shape):
@@ -96,7 +104,7 @@
     ring = take(hops - 1, 2, CHUNKS)
     ring_last = take(CHUNKS)
     xs, xr, ys = take(3)
-    back_send = take(hops, 2, CHUNKS)
+    back_send = take()
     back = take(hops - 1, 2, CHUNKS)
     back_first = take(CHUNKS)
     back_last = take(CHUNKS)
@@ -121,6 +129,7 @@
         return (zz * NX + xx, tensor)
 
     toward = [device(plane(1), x), device(plane(-1), x)]
+    toward_two = [device(plane(2), x), device(plane(-2), x)]
     along = [None] + [device(z, (x + rel) % NX) for rel in range(1, NX)]
 
     factors = [
@@ -185,10 +194,10 @@
         return ring_last[h].at[pl.ds(d * capacity[k - 1], capacity[k - 1])]
 
     def send_ring(k, d, h):
-        src = first[d][h] if k == 1 else ring_at(k - 1, d, h).at[pl.ds(0, capacity[k - 1])]
-        ring_copies[k, d, h] = remote(
-            src, ring_at(k, d, h), ring_ss.at[k - 1, d, h], ring_rs.at[k - 1, d, h], toward[d]
-        )
+        last = k == hops
+        src = first[d][h] if k == 1 else ring_at(k - 2 if last else k - 1, d, h).at[pl.ds(0, capacity[k - 1])]
+        target = toward_two[d] if last else toward[d]
+        ring_copies[k, d, h] = start(src, ring_at(k, d, h), ring_ss.at[0], ring_rs.at[k - 1, d, h], target)
 
     for h in range(CHUNKS):
         if h:
@@ -262,8 +271,10 @@
         for h in range(CHUNKS):
             for d in range(2):
                 ring_copies[k, d, h].wait_recv()
-                if k < hops:
+                if k < hops - 1:
                     send_ring(k + 1, d, h)
+                if k == hops - 2:
+                    send_ring(hops, d, h)
             ready = []
             for delta in sorted({k, planes - k}):
                 ready.append((delta, h))
@@ -321,7 +332,7 @@
         if delta == hops:
             return back_first[h], 0
         k, d = (delta, 1) if delta < hops else (planes - delta, 0)
-        return back[k - 1][d][h], capacity[k]
+        return back[k - 1][d][h], arrivals[k - 1]
 
     def send_y(delta):
         target = plane(delta)
@@ -352,37 +363,45 @@
             describe(alike, alike, y_ss.at[0], y_rs.at[delta, h], along[1]).wait_recv()
 
     back_copies = {}
+    cells_all = planes * CELLS
 
     def send_back(k, d, h):
-        if k < hops:
-            back_copies[k + 1, d, h].wait_recv()
+        for farther in [k + 1] * (k < hops - 1) + [hops] * (k == hops - 2):
+            back_copies[farther, d, h].wait_recv()
         delta = planes - k if d == 0 else k
         wait_y(delta, h)
         target_end = tab[ENDS + plane(delta)]
         low = z * CELLS
         width = capacity[k - 1]
-        filled = capacity[k] if k < hops else 0
-
+        filled = capacity[k] if k < hops - 1 else 0
         ref, row = y_at(delta, h)
+        offset = sum(capacity[: k - 1]) * 2 * CHUNKS + (d * CHUNKS + h) * width
 
         def merge(j, keep):
             rank = (target_end - 1 - j if d == 0 else target_end + j) & (nblk - 1)
             local = tab[CELL_OF + rank] - low
             at = row + jnp.clip(local, 0, CELLS - 1)
             if keep:
-                at = jnp.where((local >= 0) & (local < CELLS), at, j)
-            back_send[k - 1][d][h][j] = ref[at]
+                other = j
+                if k == hops - 2:
+                    away = lax.rem(local + cells_all, cells_all)
+                    away = away - 2 * CELLS if d == 0 else cells_all - 1 - away - CELLS
+                    two = (away >= 0) & (away < CELLS)
+                    other = jnp.where(two, filled + jnp.minimum(j, capacity[k + 1] - 1), j)
+                at = jnp.where((local >= 0) & (local < CELLS), at, other)
+            back_send[offset + j] = ref[at]
 
         loop(filled, functools.partial(merge, keep=True), 8)
         loop(width - filled, lambda j: merge(filled + j, False), 8)
-        if k > 1:
+        if k == hops:
+            landing = back[k - 3][d][h].at[pl.ds(capacity[k - 2], width)]
+        elif k > 1:
             landing = back[k - 2][d][h].at[pl.ds(0, width)]
         else:
             landing = back_last[h].at[pl.ds(d * width, width)]
-        back_copies[k, d, h] = remote(
-            back_send[k - 1][d][h], landing,
-            back_ss.at[k - 1, d, h], back_rs.at[k - 1, d, h], toward[1 - d],
-        )
+        target = toward_two[1 - d] if k == hops else toward[1 - d]
+        source = back_send.at[pl.ds(offset, width)]
+        back_copies[k, d, h] = start(source, landing, back_ss.at[0], back_rs.at[k - 1, d, h], target)
 
     points = [(k, h) for k in range(hops - 2, 1, -1) for h in range(CHUNKS)]
     points = (points[:-2] + points[-1:])[:stages]
@@ -437,9 +456,11 @@
         copy.wait_send()
     describe(xs, xs, x_ss.at[0], x_rs.at[0, 0], along[1]).wait_send()
     describe(ys, ys, y_ss.at[0], y_rs.at[0, 0], along[1]).wait_send()
-
-
-def ring_call(grad, table, left_root, right_root, planes, tensors, capacity):
+    describe(back_send, back_send, ring_ss.at[0], ring_rs.at[0, 0, 0], toward[0]).wait_send()
+    describe(back_send, back_send, back_ss.at[0], back_rs.at[0, 0, 0], toward[0]).wait_send()
+
+
+def ring_call(grad, table, left_root, right_root, planes, tensors, capacity, number):
     row_blocks, piece_rows, width = grad.shape
     nblk = row_blocks * (width // BLK)
     rows = left_root.shape[-1]
@@ -467,16 +488,16 @@
     scratch += tiles(*twice[:-2])
     scratch += tiles(2 * capacity[-1])
     scratch += [vmem((planes, CHUNKS, n, SLOTS, *tile), bf16) for n in (NX - 1, NX, NX - 1)]
-    scratch += tiles(*twice)
-    scratch += tiles(*[count + CELLS for count in twice[2:]])
+    scratch += [vmem((2 * CHUNKS * sum(capacity), *tile), bf16)]
+    scratch += tiles(*[count + CELLS for count in arrived_slots(capacity) for _ in range(2)])
     scratch += tiles(CELLS)
     scratch += tiles(2 * capacity[0] + CELLS)
     stages = (planes * NX * tensors).bit_length() - 1
     scratch += [vmem((2 * stages + 1, 8, 128), f32)]
     scratch += [dma((2,))]
-    scratch += [dma((hops, 2, CHUNKS))] * 2
+    scratch += [dma((1,)), dma((hops, 2, CHUNKS))]
     scratch += [dma((1,)), dma((planes, CHUNKS))] * 2
-    scratch += [dma((hops, 2, CHUNKS))] * 2
+    scratch += [dma((1,)), dma((hops, 2, CHUNKS))]
     scratch += [dma((stages,))] * 2
     body = functools.partial(kernel, planes, nblk, capacity)
     in_vmem = pl.BlockSpec(memory_space=pltpu.VMEM)
@@ -495,12 +516,12 @@
         out_specs=(in_vmem, pl.BlockSpec(memory_space=pltpu.SMEM)),
         scratch_shapes=scratch,
         compiler_params=pltpu.CompilerParams(
-            collective_id=0, has_side_effects=True, vmem_limit_bytes=50 * 1024 * 1024
+            collective_id=number, has_side_effects=True, vmem_limit_bytes=50 * 1024 * 1024
         ),
         cost_estimate=pl.CostEstimate(
             flops=4 * SLOTS * rows * rows * BLK, bytes_accessed=4 * 1024 * 1024, transcendentals=0
         ),
-        name="sorted_ring",
+        name=f"sorted_ring_{number}",
     )(table, grad, left_root, right_root)
 
 
@@ -539,7 +560,7 @@
     return direction.astype(jnp.bfloat16), update_rms
 
 
-def per_device(capacity, grad, owner, left_root, right_root):
+def per_device(capacities, grad, owner, left_root, right_root):
     row_blocks, piece_rows, width = grad.shape
     dp_size = lax.axis_size("dp")
     tensors = lax.axis_size("tensor")
@@ -547,25 +568,26 @@
     col_blocks = width // BLK
     tensor_index = lax.axis_index("tensor")
     here = lax.dynamic_slice_in_dim(owner, tensor_index * col_blocks, col_blocks, 1).reshape(-1)
-    ends, ups, fits = plane_split(owner, tensors, planes, capacity)
+    ends, ups, level = plane_split(owner, tensors, planes, capacities)
     cell, rank = block_cells(here)
     ends = lax.dynamic_index_in_dim(ends, tensor_index, 0, keepdims=False)
     ups = lax.dynamic_index_in_dim(ups, tensor_index, 0, keepdims=False)
     table = make_table(cell, rank, ends, ups, dp_size)
 
-    def fast(grad, table, cell, left_root, right_root):
-        moved, rms = ring_call(grad, table, left_root, right_root, planes, tensors, capacity)
+    def sorted_lists(number, grad, table, cell, left_root, right_root):
+        moved, rms = ring_call(grad, table, left_root, right_root, planes, tensors, capacities[number], number)
         return moved, rms.reshape(())
 
     def padded(grad, table, cell, left_root, right_root):
         return padded_call(grad, cell, left_root, right_root, dp_size)
 
-    return lax.cond(fits, fast, padded, grad, table, cell, left_root, right_root)
-
-
-def build(mesh, capacity):
+    branches = [functools.partial(sorted_lists, number) for number in range(len(capacities))] + [padded]
+    return lax.switch(level, branches, grad, table, cell, left_root, right_root)
+
+
+def build(mesh, capacities):
     return jax.shard_map(
-        functools.partial(per_device, capacity),
+        functools.partial(per_device, capacities),
         mesh=mesh,
         in_specs=(
             P(None, "dp", "tensor"),
@@ -579,4 +601,4 @@
 
 
 def solution(mesh):
-    return build(mesh, CAPACITY)
+    return build(mesh, CAPACITIES)

time: 120 us -> 117 us (0.975)
  Pallas kernels: 110 us -> 107 us
    pallas_call x1, Pallas kernels: 110 us -> 107 us  [ring_call(): pl.pallas_call(body, out_shape=(jax.ShapeDtypeStruct(grad.shape, bf16), j...]
where the time goes in v4:
time: 117 us; the launch traced here: 115 us
  Pallas kernels  107 us (91%)
  between operations  3.1 us (3%)
  other arithmetic  2.23 us (2%)
  local copies, waits for them, and re-layouts  1.82 us (2%)
    pallas_call x1, Pallas kernels, ring_call(): pl.pallas_call(body, out_shape=(jax.ShapeDtypeStruct(grad.shape, bf16), j...  107 us

profile of v4, /device:TPU:1, one launch (start us, length us, event | category | flops | bytes accessed | tf_op | source)
XLA Modules:
  0.0 114.8 jit_solution(7895508924065396565)
XLA Ops:
  0.6 0.8 constant_dynamic-slice_fusion.2
  1.4 0.1 reshape.90
  1.5 0.2 convert_reduce_fusion.3
  1.7 0.2 convert_reduce_fusion.2
  1.9 0.1 select_reduce_fusion
  2.0 0.7 add_select_fusion
  2.7 0.1 copy.31
  2.8 0.2 convolution_convert_fusion.4
  3.0 0.1 maximum_maximum_fusion.1
  3.1 0.1 maximum_maximum_fusion
  3.2 0.1 slice_subtract_fusion
  3.3 0.1 convert_reduce_fusion.1
  3.4 0.1 concatenate.3
  3.5 0.6 select_reduce_fusion.2
  4.8 107.4 %conditional.1 = (bf16[16,8,2048]{2,1,0:T(8,128)(2,1)S(1)}, f32[]{:T(128)}) conditional(s32[]{:T(128)} %clamp.3, (s32[416]{0:T(512)S(1)}, bf16[16,8,2048]{2,1,0:T(8,128)(2,1)}, bf16[1,3,512,512]{3,2,1,0:T(8,128)(2,1)}, bf16[1,3,512,512]{3,2,1,0:T(8,128)(2,1)}) %tuple.19, (s32[416]{0:T(512)S(1)}, bf16[16,8,2048]{2,1,0:T(8,128)(2,1)}, ...), branch_computations={%region_8.9_spmd, %region_9.10_spmd, %region_10.21_spmd} | conditional | flops 1722563072 | bytes 51387028 | solution.py:585
  5.0 107.0 %sorted_ring_1.1 = (bf16[16,8,2048]{2,1,0:T(8,128)(2,1)S(1)}, f32[1,1]{1,0:T(1,128)}) custom-call(s32[416]{0:T(512)S(1)} %get-tuple-element.36.refs_0_, bf16[16,8,2048]{2,1,0:T(8,128)(2,1)} %get-tuple-element.37.refs_1_, bf16[1,3,512,512]{3,2,1,0:T(8,128)(2,1)} %get-tuple-element.38.refs_2_, bf16[1,3,512,512]{3,2,1,0:T(8,128)(2,1)} %get-tuple-element.39.refs_3_), custom_call_target="tpu_custom_call" | custom-call | flops 1610612736 | bytes 4194304 | tf_op jit(solution)/shard_map/cond/branch_1_fun/sorted_ring_1/pallas_call | solution.py:504
  112.2 0.8 copy.68
  (5 shorter events, 0.1 us)

commit v5 on v4

--- a/solution.py
+++ b/solution.py
@@ -16,7 +16,6 @@
 CELLS = NX * SLOTS
 CHUNKS = 2
 BITS = (1, 2, 4, 8, 16, 32)
-DISTANCE = ((0, 1, 2, 0, 0, 0), (1, 2, 1, 2, 4, 8))
 CAPACITIES = ((38, 34, 30, 25, 20, 15, 10, 5), (42, 37, 34, 28, 24, 19, 12, 7))
 
 
@@ -96,9 +95,9 @@
             return next(names)
         return [take(*shape[1:]) for _ in range(shape[0])]
 
-    tab, grad, left_hbm, right_hbm = take(4)
+    tab_hbm, grad_hbm, left_hbm, right_hbm = take(4)
     out, rms_out = take(2)
-    left, right, mats, halves, prods, scales, squares = take(7)
+    tab, grad, left, right, mats, halves, prods, scales, squares = take(9)
     folded = take(CHUNKS)
     first = take(2, CHUNKS)
     ring = take(hops - 1, 2, CHUNKS)
@@ -136,13 +135,17 @@
         pltpu.make_async_copy(left_hbm.at[0], left, load_sem.at[0]),
         pltpu.make_async_copy(right_hbm.at[0], right, load_sem.at[1]),
     ]
-    for copy in factors:
+    inputs = [
+        pltpu.make_async_copy(tab_hbm, tab, load_sem.at[2]),
+        pltpu.make_async_copy(grad_hbm, grad, load_sem.at[3]),
+    ]
+    for copy in inputs + factors:
         copy.start()
 
     barrier = pltpu.get_barrier_semaphore()
     partners = []
-    bits = [(stride, place) for place, size in ((0, tensors), (1, devices)) for stride in BITS if stride < size]
-    for stride, place in sorted(bits, key=lambda bit: (DISTANCE[bit[1]][BITS.index(bit[0])], bit)):
+    bits = [(place, stride) for place, size in ((0, tensors), (1, devices)) for stride in BITS if stride < size]
+    for place, stride in reversed(bits):
         if place:
             partners.append((dp + stride - 2 * stride * ((dp // stride) % 2), tensor))
         else:
@@ -151,6 +154,8 @@
     for peer in peers:
         pl.semaphore_signal(barrier, inc=1, device_id=peer, device_id_type=MESH)
 
+    for copy in inputs:
+        copy.wait()
     end = tab[ENDS + z]
 
     def fill_chunk(h):
@@ -294,7 +299,8 @@
             halves[s, :, pl.ds(h * 256, 256)] = part.astype(jnp.bfloat16)
             return carry
 
-        lax.fori_loop(0, SLOTS, left_part, 0)
+        for s in range(SLOTS):
+            left_part(s, 0)
 
     cells = rows * BLK
 
@@ -310,7 +316,9 @@
         held = found == jnp.full((1, 1), dp * SLOTS + s)
         return total + jnp.where(held, prod_sum * scale * scale, 0.0)
 
-    total = lax.fori_loop(0, SLOTS, right_part, jnp.zeros((1, 1), jnp.float32))
+    total = jnp.zeros((1, 1), jnp.float32)
+    for s in range(SLOTS):
+        total = right_part(s, total)
     stages = len(partners)
     sums[0] = jnp.broadcast_to(total, sums.shape[1:])
     sum_copies = []
@@ -403,8 +411,9 @@
         source = back_send.at[pl.ds(offset, width)]
         back_copies[k, d, h] = start(source, landing, back_ss.at[0], back_rs.at[k - 1, d, h], target)
 
-    points = [(k, h) for k in range(hops - 2, 1, -1) for h in range(CHUNKS)]
-    points = (points[:-2] + points[-1:])[:stages]
+    points = [(hops, 0)] + [(k, 1) for k in range(hops - 2, max(hops - 5, 0), -1)]
+    points += [(k, h) for k in range(hops - 5, 0, -1) for h in range(CHUNKS)]
+    points = points[:stages]
     sent = set()
 
     def ensure_y(delta):
@@ -474,6 +483,8 @@
         return [vmem((count, *tile), bf16) for count in counts for _ in range(CHUNKS)]
 
     scratch = [
+        pltpu.SMEM(table.shape, jnp.int32),
+        vmem(grad.shape, bf16),
         vmem((SLOTS, rows, rows), bf16),
         vmem((SLOTS, BLK, BLK), bf16),
         vmem((SLOTS, rows, BLK), bf16),
@@ -494,7 +505,7 @@
     scratch += tiles(2 * capacity[0] + CELLS)
     stages = (planes * NX * tensors).bit_length() - 1
     scratch += [vmem((2 * stages + 1, 8, 128), f32)]
-    scratch += [dma((2,))]
+    scratch += [dma((4,))]
     scratch += [dma((1,)), dma((hops, 2, CHUNKS))]
     scratch += [dma((1,)), dma((planes, CHUNKS))] * 2
     scratch += [dma((1,)), dma((hops, 2, CHUNKS))]
@@ -508,8 +519,8 @@
             jax.ShapeDtypeStruct((1, 1), f32),
         ),
         in_specs=[
-            pl.BlockSpec(memory_space=pltpu.SMEM),
-            in_vmem,
+            pl.BlockSpec(memory_space=pl.ANY),
+            pl.BlockSpec(memory_space=pl.ANY),
             pl.BlockSpec(memory_space=pl.ANY),
             pl.BlockSpec(memory_space=pl.ANY),
         ],

time: 117 us -> 108 us (0.923)
  the two profiles are of different devices: /device:TPU:1 before, /device:TPU:2 now
where the time goes in v5:
time: 108 us
  Pallas kernels  100 us (93%)
  between operations  3.1 us (3%)
  other arithmetic  2.23 us (2%)
  local copies, waits for them, and re-layouts  1.82 us (2%)
    pallas_call x1, Pallas kernels, ring_call(): pl.pallas_call(body, out_shape=(jax.ShapeDtypeStruct(grad.shape, bf16), j...  100 us

profile of v5, /device:TPU:2, one launch (start us, length us, event | category | flops | bytes accessed | tf_op | source)
XLA Modules:
  0.0 107.8 jit_solution(8117942719008085837)
XLA Ops:
  0.6 0.8 constant_dynamic-slice_fusion.2
  1.4 0.1 reshape.90
  1.5 0.2 convert_reduce_fusion.3
  1.7 0.2 convert_reduce_fusion.2
  1.9 0.1 select_reduce_fusion
  2.0 0.7 add_select_fusion
  2.7 0.1 copy.31
  2.8 0.2 convolution_convert_fusion.4
  3.0 0.1 maximum_maximum_fusion.1
  3.1 0.1 maximum_maximum_fusion
  3.2 0.1 slice_subtract_fusion
  3.3 0.1 convert_reduce_fusion.1
  3.4 0.1 concatenate.3
  3.5 0.6 select_reduce_fusion.2
  4.8 100.5 %conditional.1 = (bf16[16,8,2048]{2,1,0:T(8,128)(2,1)S(1)}, f32[]{:T(128)}) conditional(s32[]{:T(128)} %clamp.3, (s32[416]{0:T(512)S(1)}, bf16[16,8,2048]{2,1,0:T(8,128)(2,1)}, bf16[1,3,512,512]{3,2,1,0:T(8,128)(2,1)}, bf16[1,3,512,512]{3,2,1,0:T(8,128)(2,1)}) %tuple.19, (s32[416]{0:T(512)S(1)}, bf16[16,8,2048]{2,1,0:T(8,128)(2,1)}, ...), branch_computations={%region_8.9_spmd, %region_9.10_spmd, %region_10.21_spmd} | conditional | flops 1722563072 | bytes 51387028 | solution.py:596
  4.8 100.3 %sorted_ring_0.1 = (bf16[16,8,2048]{2,1,0:T(8,128)(2,1)S(1)}, f32[1,1]{1,0:T(1,128)}) custom-call(s32[416]{0:T(512)S(1)} %get-tuple-element.30.refs_0_, bf16[16,8,2048]{2,1,0:T(8,128)(2,1)} %get-tuple-element.31.refs_1_, bf16[1,3,512,512]{3,2,1,0:T(8,128)(2,1)} %get-tuple-element.32.refs_2_, bf16[1,3,512,512]{3,2,1,0:T(8,128)(2,1)} %get-tuple-element.33.refs_3_), custom_call_target="tpu_custom_call" | custom-call | flops 1610612736 | bytes 4194304 | tf_op jit(solution)/shard_map/cond/branch_0_fun/sorted_ring_0/pallas_call | solution.py:515
  105.3 0.8 copy.68
  (5 shorter events, 0.1 us)

commit v6 on v5

--- a/solution.py
+++ b/solution.py
@@ -49,18 +49,18 @@
         fits = low <= high
         level = jnp.where(fits, i, level)
         ends = jnp.where(fits, jnp.maximum((high + low) // 2, first), ends)
-    return ends, ends - first, jnp.max(level)
-
-
-def make_table(cell, rank, ends, ups, devices):
+    return ends, jnp.max(level)
+
+
+def make_table(cell, rank, ends, devices):
     n = cell.shape[0]
     index = jnp.arange(n, dtype=jnp.int32)
     hit = (rank[None, :] == index[:, None]).astype(jnp.int32)
     block_of = jnp.sum(hit * index[None, :], axis=-1)
     cell_of = jnp.sum(hit * cell[None, :], axis=-1)
-    cells = jnp.arange(devices * SLOTS, dtype=jnp.int32)
+    cells = jnp.arange(devices * SLOTS + 1, dtype=jnp.int32)
     below = jnp.sum((cell[None, :] < cells[:, None]).astype(jnp.int32), axis=-1)
-    return jnp.concatenate([block_of, cell_of, rank, below, ends, ups])
+    return jnp.concatenate([block_of, cell_of, rank, below, ends])
 
 
 def fold(piece):
@@ -118,8 +118,7 @@
     devices = planes * NX
     per_row = nblk // grad.shape[0]
     CELL_OF, RANK_OF, BELOW = nblk, 2 * nblk, 3 * nblk
-    ENDS = BELOW + devices * SLOTS
-    UPS = ENDS + planes
+    ENDS = BELOW + devices * SLOTS + 1
 
     def plane(delta):
         return (z + (delta + planes)) % planes
@@ -234,7 +233,8 @@
 
     def pick(delta, h):
         source = plane(-delta)
-        source_end, source_ups = tab[ENDS + source], tab[UPS + source]
+        source_end = tab[ENDS + source]
+        source_ups = source_end - tab[BELOW + (source + 1) * CELLS]
         k = min(delta, planes - delta)
         room = capacity[k - 1]
         for rel in range(NX):
@@ -439,7 +439,7 @@
     inv_rms = (1.0 / update_rms)[:1, :1]
 
     end = tab[ENDS + z]
-    ups = tab[UPS + z]
+    ups = end - tab[BELOW + (z + 1) * CELLS]
     for h in range(CHUNKS):
         for d in range(2):
             back_copies[1, d, h].wait_recv()
@@ -459,7 +459,7 @@
             column = (b % per_row) * BLK + h * 256
             out[b // per_row, :, pl.ds(pl.multiple_of(column, 256), 256)] = wide
 
-        loop(nblk, finish, 8)
+        loop(nblk, finish, 16)
 
     for copy in sends:
         copy.wait_send()
@@ -579,11 +579,10 @@
     col_blocks = width // BLK
     tensor_index = lax.axis_index("tensor")
     here = lax.dynamic_slice_in_dim(owner, tensor_index * col_blocks, col_blocks, 1).reshape(-1)
-    ends, ups, level = plane_split(owner, tensors, planes, capacities)
+    ends, level = plane_split(owner, tensors, planes, capacities)
     cell, rank = block_cells(here)
     ends = lax.dynamic_index_in_dim(ends, tensor_index, 0, keepdims=False)
-    ups = lax.dynamic_index_in_dim(ups, tensor_index, 0, keepdims=False)
-    table = make_table(cell, rank, ends, ups, dp_size)
+    table = make_table(cell, rank, ends, dp_size)
 
     def sorted_lists(number, grad, table, cell, left_root, right_root):
         moved, rms = ring_call(grad, table, left_root, right_root, planes, tensors, capacities[number], number)

time: 108 us -> 110 us (1.019); the launches traced: 108 us -> 112 us
  Pallas kernels: 100 us -> 105 us
    pallas_call x1, Pallas kernels: 100 us -> 105 us  [ring_call(): pl.pallas_call(body, out_shape=(jax.ShapeDtypeStruct(grad.shape, bf16), j...]
where the time goes in v6:
time: 110 us; the launch traced here: 112 us
  Pallas kernels  105 us (95%)
  between operations  3.1 us (3%)
  other arithmetic  2.23 us (2%)
  local copies, waits for them, and re-layouts  1.82 us (2%)
    pallas_call x1, Pallas kernels, ring_call(): pl.pallas_call(body, out_shape=(jax.ShapeDtypeStruct(grad.shape, bf16), j...  105 us

profile of v6, /device:TPU:2, one launch (start us, length us, event | category | flops | bytes accessed | tf_op | source)
XLA Modules:
  0.0 112.3 jit_solution(9949757720740228443)
XLA Ops:
  0.6 0.8 constant_dynamic-slice_fusion
  1.4 0.1 reshape.90
  1.5 0.2 convert_reduce_fusion.3
  1.7 0.2 convert_reduce_fusion.2
  1.9 0.1 select_reduce_fusion
  2.0 0.1 convert_reduce_fusion.1
  2.1 0.7 add_select_fusion
  2.8 0.1 copy.31
  2.9 0.2 convolution_convert_fusion.4
  3.1 0.1 maximum_maximum_fusion.1
  3.2 0.1 maximum_maximum_fusion
  3.3 0.1 fusion.35
  3.4 0.1 concatenate.3
  3.5 0.6 select_reduce_fusion.2
  4.8 104.9 %conditional.1 = (bf16[16,8,2048]{2,1,0:T(8,128)(2,1)S(1)}, f32[]{:T(128)}) conditional(s32[]{:T(128)} %clamp.3, (s32[401]{0:T(512)S(1)}, bf16[16,8,2048]{2,1,0:T(8,128)(2,1)}, bf16[1,3,512,512]{3,2,1,0:T(8,128)(2,1)}, bf16[1,3,512,512]{3,2,1,0:T(8,128)(2,1)}) %tuple.19, (s32[401]{0:T(512)S(1)}, bf16[16,8,2048]{2,1,0:T(8,128)(2,1)}, ...), branch_computations={%region_8.9_spmd, %region_9.10_spmd, %region_10.21_spmd} | conditional | flops 1722563072 | bytes 51387028 | solution.py:595
  5.0 104.5 %sorted_ring_1.1 = (bf16[16,8,2048]{2,1,0:T(8,128)(2,1)S(1)}, f32[1,1]{1,0:T(1,128)}) custom-call(s32[401]{0:T(512)S(1)} %get-tuple-element.36.refs_0_, bf16[16,8,2048]{2,1,0:T(8,128)(2,1)} %get-tuple-element.37.refs_1_, bf16[1,3,512,512]{3,2,1,0:T(8,128)(2,1)} %get-tuple-element.38.refs_2_, bf16[1,3,512,512]{3,2,1,0:T(8,128)(2,1)} %get-tuple-element.39.refs_3_), custom_call_target="tpu_custom_call" | custom-call | flops 1610612736 | bytes 4194304 | tf_op jit(solution)/shard_map/cond/branch_1_fun/sorted_ring_1/pallas_call | solution.py:515
  109.7 0.8 copy.68
  (5 shorter events, 0.1 us)
